TPU v7x, 32 devices: a whole 2x2x4 slice. The times are simulated.
32 devices in a mesh: enc: 4 (over y, x), seq: 8 (over z, core).
Axes of the slice: x: 2, y: 2, z: 4, core: 2. Of those that a mesh axis runs over, the one named last changes fastest.
Arguments:
- qkv: bfloat16 [16, 512, 3840], P('enc', 'seq'), may hold values from -6 to 6
- resid: bfloat16 [16, 512, 1280], P('enc', 'seq'), may hold values from -6 to 6
- block_count: int32 [4, 8], P('enc', 'seq'), may hold values from 2 to 4, as said below
- send_count: int32 [4, 8], P('enc', 'seq'), may hold values from 0 to 1, as said below
- send_slot: int32 [4, 384], P('enc', 'seq'), may hold values from 0 to 47, as said below
- lm_row: int32 [4, 384], P('enc', 'seq'), may hold values from -1 to 47, as said below
- out_weight: bfloat16 [1280, 1280], replicated, may hold values from -0.15625 to 0.15625
- out_bias: bfloat16 [1280], replicated, may hold values from -3 to 3
- norm_gain: bfloat16 [1280], replicated, may hold values from 0.25 to 1.75
Outputs:
- lm_tokens: bfloat16 [4, 384, 5120], P('enc', 'seq')
Inputs may be any that keep to these rules, and one draw needn't show every extreme that they name: send_count is at most 1; a device's live slots come first. block_count[e, g] = 3 + send_count[e, g] - send_count[(e - 1) mod 4, g]. `send_slot`: values of one device are distinct; with o = (s - g) mod 8 and finv(o) = 2 * o for o < 4, else 2 * (o - 4) + 1, the device at seq index g uses slot s * 6 + k exactly when k * 8 + finv(o) < 48. `lm_row`: at seq index s, with o and finv as for send_slot, arriving slot g * 6 + k holds -1 exactly when k * 8 + finv((s - g) mod 8) >= 48; the other slots hold each of 0 to 47 once.
All inputs are finite; a program needn't handle non-finite values.
Results may differ from a plain program's by a relative error of at most 0.0036.
Values may be sent and summed in bfloat16 or wider, within the bound.
No kernel may reach another device: no remote copies, remote signals or barrier semaphores. Data moves between devices by JAX's collectives and lax.ppermute only.
A program may use at most 64 MiB of HBM per device.

v0:
```python
import functools
import math

import jax
import jax.numpy as jnp
from jax import lax
from jax.experimental import pallas as pl
from jax.experimental.pallas import tpu as pltpu
from jax.sharding import PartitionSpec as P

HEADS = 16
WIN = 64
LANES = 128
GROUP = 4
EPS = 1e-6
CORES = 2

NT = (((1,), (1,)), ((), ()))


def dot32(a, b):
    return jnp.dot(a, b, preferred_element_type=jnp.float32)


def one_hot(match):
    return match.astype(jnp.float32).astype(jnp.bfloat16)


def attend(q, k, v, out_ref, row0, width):
    head = width // HEADS
    rate = 1.0 / math.sqrt(head)
    totals = [None] * (width // LANES)
    sums = [None] * (width // LANES)
    first_half = lax.broadcasted_iota(jnp.int32, (WIN, 2 * WIN), 1) < WIN
    for pair in range(HEADS // 2):
        start = 2 * pair * head
        lo = start // LANES * LANES
        hi = -(-(start + 2 * head) // LANES) * LANES
        column = lax.broadcasted_iota(jnp.int32, (2 * WIN, hi - lo), 1) + lo
        row = lax.broadcasted_iota(jnp.int32, (2 * WIN, hi - lo), 0)
        begin = jnp.where(row < WIN, start, start + head)
        mask = one_hot((column >= begin) & (column < begin + head))
        kw, vw = k(lo, hi), v(lo, hi)
        keys = jnp.concatenate([kw, kw], axis=0) * mask
        values = jnp.concatenate([vw, vw], axis=0) * mask
        scores = lax.dot_general(q(lo, hi), keys, NT, preferred_element_type=jnp.float32)
        top0 = jnp.max(jnp.where(first_half, scores, -jnp.inf), axis=1, keepdims=True)
        top1 = jnp.max(jnp.where(first_half, -jnp.inf, scores), axis=1, keepdims=True)
        raised = jnp.exp((scores - jnp.where(first_half, top0, top1)) * rate).astype(jnp.bfloat16)
        part = dot32(raised, values)
        norm = dot32(raised, mask)
        for tile in range(lo // LANES, hi // LANES):
            at = slice(tile * LANES - lo, (tile + 1) * LANES - lo)
            totals[tile] = part[:, at] if totals[tile] is None else totals[tile] + part[:, at]
            sums[tile] = norm[:, at] if sums[tile] is None else sums[tile] + norm[:, at]
    for tile in range(width // LANES):
        out_ref[row0 : row0 + WIN, tile * LANES : (tile + 1) * LANES] = (totals[tile] / sums[tile]).astype(
            jnp.bfloat16
        )


def attend_all(qkv, attended, width):
    for b in range(qkv.shape[0]):
        attend(
            lambda lo, hi, b=b: qkv[b, :, lo:hi],
            lambda lo, hi, b=b: qkv[b, :, width + lo : width + hi],
            lambda lo, hi, b=b: qkv[b, :, 2 * width + lo : 2 * width + hi],
            attended, b * WIN, width,
        )


def project(attended, resid, weight, bias, gain, hidden, out_ref):
    rows, width = hidden.shape
    step = 2 * LANES
    chunks = [slice(lo, lo + step) for lo in range(0, width, step)]
    squares = jnp.zeros((rows, 1), jnp.float32)
    for cols in chunks:
        h = dot32(attended[...], weight[:, cols])
        h = h + bias[cols].astype(jnp.float32).reshape(1, step)
        h = h + resid[:, :, cols].reshape(rows, step).astype(jnp.float32)
        hidden[:, cols] = h
        squares = squares + jnp.sum(h * h, axis=1, keepdims=True)
    scale = lax.rsqrt(squares * (1.0 / width) + EPS)
    for cols in chunks:
        out_ref[:, cols] = (hidden[:, cols] * scale * gain[cols].astype(jnp.float32).reshape(1, step)).astype(jnp.bfloat16)


def lent_kernel(
    count_ref, qkv_hbm, resid_hbm, weight_hbm, bias_hbm, gain_hbm, out_ref,
    qkv, resid, weight, attended, hidden, bias, gain, sems, weight_sems,
):
    width = resid.shape[2]
    at = pl.ds(count_ref[0, 0] - 1, 1)
    step = width // weight_sems.shape[0]
    chunks = [slice(lo, lo + step) for lo in range(0, width, step)]
    qkv_copy = pltpu.make_async_copy(qkv_hbm.at[at], qkv, sems.at[0])
    weight_copies = [
        pltpu.make_async_copy(weight_hbm.at[part], weight.at[part], weight_sems.at[i]) for i, part in enumerate(chunks)
    ]
    pairs = [(resid_hbm.at[at], resid), (bias_hbm, bias), (gain_hbm, gain)]
    other_copies = [pltpu.make_async_copy(a, b, sems.at[i + 1]) for i, (a, b) in enumerate(pairs)]
    for copy in [qkv_copy] + weight_copies[:-1] + other_copies + weight_copies[-1:]:
        copy.start()
    qkv_copy.wait()
    attend_all(qkv, attended, width)
    for copy, part in list(zip(weight_copies, chunks))[:-1]:
        copy.wait()
        for cols in chunks:
            h = dot32(attended[:, part], weight[part, cols])
            hidden[:, cols] = h if part.start == 0 else hidden[:, cols] + h
    for copy in other_copies:
        copy.wait()
    for cols in chunks:
        h = hidden[:, cols] + bias[cols].astype(jnp.float32).reshape(1, step)
        hidden[:, cols] = h + resid[0, :, cols].astype(jnp.float32)
    weight_copies[-1].wait()
    squares = jnp.zeros((WIN, 1), jnp.float32)
    for cols in chunks:
        h = hidden[:, cols] + dot32(attended[:, chunks[-1]], weight[chunks[-1], cols])
        hidden[:, cols] = h
        squares = squares + jnp.sum(h * h, axis=1, keepdims=True)
    scale = lax.rsqrt(squares * (1.0 / width) + EPS)
    for cols in chunks:
        out_ref[:, cols] = (hidden[:, cols] * scale * gain[cols].astype(jnp.float32).reshape(1, step)).astype(jnp.bfloat16)


def encode(qkv_hbm, resid_hbm, weight_hbm, bias_hbm, gain_hbm, out_ref, qkv, resid, weight, attended, hidden, bias, gain, sems):
    at = pl.ds(0, qkv.shape[0])
    pairs = [(qkv_hbm.at[at], qkv), (weight_hbm, weight), (resid_hbm.at[at], resid), (bias_hbm, bias), (gain_hbm, gain)]
    copies = [pltpu.make_async_copy(a, b, sems.at[i]) for i, (a, b) in enumerate(pairs)]
    for copy in copies:
        copy.start()
    copies[0].wait()
    attend_all(qkv, attended, resid.shape[2])
    for copy in copies[1:]:
        copy.wait()
    project(attended, resid, weight, bias, gain, hidden, out_ref)


def split_index(index, n_seq, cap):
    step = index // (GROUP * cap)
    rest = index - step * (GROUP * cap)
    patch = rest // cap
    return step, patch, rest - patch * cap


def own_kernel(
    n_seq, cap, peer, count_ref, send_ref, me_ref, slot_ref, row_ref,
    qkv_hbm, resid_hbm, weight_hbm, bias_hbm, gain_hbm,
    packed_ref, borrow_ref, place_ref, normed, *scratch,
):
    rows = normed.shape[0]
    slots = n_seq * cap
    sent = slots * GROUP
    tokens = rows // GROUP
    me = me_ref[0, 0]
    encode(qkv_hbm, resid_hbm, weight_hbm, bias_hbm, gain_hbm, normed, *scratch)

    step, patch, rank = split_index(lax.broadcasted_iota(jnp.int32, (sent, 1), 0), n_seq, cap)
    row_code = (peer(me, step, 1) * cap + rank) * GROUP + patch
    token = lax.broadcasted_iota(jnp.int32, (tokens, rows), 0)
    column = lax.broadcasted_iota(jnp.int32, (tokens, rows), 1)
    spread = one_hot((column >= token * GROUP) & (column < (token + 1) * GROUP))
    slot = jnp.broadcast_to(slot_ref[...].astype(jnp.float32), (16, tokens)).astype(jnp.bfloat16)
    slot = dot32(slot, spread)[:1].astype(jnp.int32)
    index = lax.broadcasted_iota(jnp.int32, (1, rows), 1)
    col_code = slot * GROUP + jnp.bitwise_and(index, GROUP - 1)
    kept = (count_ref[0, 0] - send_ref[0, 0]) * WIN
    last = rows - WIN
    own = one_hot(row_code == jnp.where(index < kept, col_code, -1))
    packed_ref[...] = dot32(own, normed[...]).astype(jnp.bfloat16)
    borrow_ref[...] = one_hot(row_code == jnp.where(kept > last, -1, col_code[:, last:]))

    step, patch, rank = split_index(lax.broadcasted_iota(jnp.int32, (1, sent), 1), n_seq, cap)
    arrive = peer(me, step, -1) * cap + rank
    pick = one_hot(lax.broadcasted_iota(jnp.int32, (slots, sent), 0) == arrive)
    target = jnp.broadcast_to(row_ref[...].astype(jnp.float32), (16, slots)).astype(jnp.bfloat16)
    target = dot32(target, pick)[:1].astype(jnp.int32)
    out_row = lax.broadcasted_iota(jnp.int32, (tokens, sent), 0)
    for j in range(GROUP):
        place_ref[j * tokens : (j + 1) * tokens, :] = one_hot((target == out_row) & (patch == j))


def in_hbm(*arrays):
    return [pltpu.with_memory_space_constraint(a, pltpu.HBM) for a in arrays]


def encode_call(kernel, blocks, scalars, slots, qkv, resid, weight, bias, gain, out_shape, before=(), after=()):
    width = resid.shape[2]
    rows = blocks * WIN
    vmem = pl.BlockSpec(memory_space=pltpu.VMEM)
    smem = pl.BlockSpec(memory_space=pltpu.SMEM)
    hbm = pl.BlockSpec(memory_space=pltpu.HBM)
    return pl.pallas_call(
        kernel,
        out_shape=out_shape,
        in_specs=[smem] * len(scalars) + [vmem] * len(slots) + [hbm] * 5,
        out_specs=jax.tree.map(lambda _: vmem, out_shape),
        scratch_shapes=[
            *before,
            pltpu.VMEM((blocks, WIN, 3 * width), jnp.bfloat16),
            pltpu.VMEM((blocks, WIN, width), jnp.bfloat16),
            pltpu.VMEM((width, width), jnp.bfloat16),
            pltpu.VMEM((rows, width), jnp.bfloat16),
            pltpu.VMEM((rows, width), jnp.float32),
            pltpu.VMEM((width,), jnp.bfloat16),
            pltpu.VMEM((width,), jnp.bfloat16),
            pltpu.SemaphoreType.DMA((5,)),
            *after,
        ],
        compiler_params=pltpu.CompilerParams(vmem_limit_bytes=24 << 20),
        cost_estimate=pl.CostEstimate(
            flops=2 * rows * width * width + 8 * rows * WIN * width,
            bytes_accessed=2 * (width * width + 5 * rows * width),
            transcendentals=rows * WIN * HEADS,
        ),
    )(*scalars, *slots, *in_hbm(qkv, resid, weight, bias, gain))


def pack_kernel(packed_ref, borrow_ref, borrowed_ref, *out_refs):
    total = packed_ref[...].astype(jnp.float32) + dot32(borrow_ref[...], borrowed_ref[...])
    chunk = out_refs[0].shape[0]
    for step, out_ref in enumerate(out_refs):
        out_ref[...] = total[step * chunk : (step + 1) * chunk].astype(jnp.bfloat16)


def place_kernel(place_ref, *refs):
    *in_refs, out_hbm, out, sems = refs
    tokens = out.shape[0]
    chunks = [ref[...].astype(jnp.float32) for ref in in_refs]
    arrived = chunks[0] if len(chunks) == 1 else jnp.concatenate(chunks, axis=0)
    arrived = arrived.astype(jnp.bfloat16)
    width = arrived.shape[1]
    copies = []
    for j in range(GROUP):
        cols = slice(j * width, (j + 1) * width)
        out[:, cols] = dot32(place_ref[j * tokens : (j + 1) * tokens, :], arrived).astype(jnp.bfloat16)
        copies.append(pltpu.make_async_copy(out.at[:, cols], out_hbm.at[:, cols], sems.at[j]))
        copies[-1].start()
    for copy in copies:
        copy.wait()


def exchange_steps(n_seq):
    n_z = n_seq // CORES
    steps = [(dz, dc) for dz in range(n_z) for dc in range(CORES) if (dz, dc) != (0, 0)]
    return [(0, 0)] + sorted(steps, key=lambda s: (abs(s[0] - n_z / 2), s[1], s[0]))


def chip_peer(n_seq, me, step, sign):
    n_z = n_seq // CORES
    offset = jnp.zeros_like(step)
    flip = jnp.zeros_like(step)
    for i, (dz, dc) in enumerate(exchange_steps(n_seq)):
        offset = jnp.where(step == i, dz, offset)
        flip = jnp.where(step == i, dc, flip)
    z = me // CORES + sign * offset
    z = jnp.where(z >= n_z, z - n_z, jnp.where(z < 0, z + n_z, z))
    return z * CORES + jnp.bitwise_xor(jnp.bitwise_and(me, 1), flip)


def per_device(
    qkv, resid, block_count, send_count, send_slot, lm_row, out_weight, out_bias, norm_gain
):
    width = resid.shape[2]
    row_total = send_slot.shape[1]
    tokens = WIN // GROUP
    blocks = row_total // tokens
    n_seq = lax.axis_size("seq")
    n_enc = lax.axis_size("enc")
    slots = lm_row.shape[1]
    cap = slots // n_seq
    chunk = GROUP * cap
    sent = slots * GROUP
    vmem = pl.BlockSpec(memory_space=pltpu.VMEM)
    small = pltpu.CompilerParams(vmem_limit_bytes=16 << 20)

    def rows_of(count, columns=width):
        return jax.ShapeDtypeStruct((count, columns), jnp.bfloat16)

    data = (qkv, resid, out_weight, out_bias, norm_gain)
    weight_parts = [pltpu.SemaphoreType.DMA((width // (2 * LANES),))]
    lent = encode_call(lent_kernel, 1, [block_count], [], *data, rows_of(WIN), after=weight_parts)
    borrowed = lax.ppermute(lent, "enc", [((i - 1) % n_enc, i) for i in range(n_enc)])

    by_steps = chunk % 8 == 0 and n_seq % CORES == 0
    peer = functools.partial(chip_peer, n_seq) if by_steps else lambda me, step, sign: step
    me = lax.axis_index("seq").astype(jnp.int32).reshape(1, 1)
    packed, borrow, place = encode_call(
        functools.partial(own_kernel, n_seq, cap, peer), blocks,
        [block_count, send_count, me], [send_slot, lm_row], *data,
        (rows_of(sent), rows_of(sent, WIN), rows_of(GROUP * row_total, sent)),
        [pltpu.VMEM((row_total * GROUP, width), jnp.bfloat16)],
    )
    pieces = n_seq if by_steps else 1
    outgoing = pl.pallas_call(
        pack_kernel,
        out_shape=[rows_of(sent // pieces)] * pieces,
        in_specs=[vmem] * 3,
        out_specs=[vmem] * pieces,
        compiler_params=small,
    )(packed, borrow, borrowed)

    if by_steps:
        n_z = n_seq // CORES
        arrived = [outgoing[0]]
        for part, (dz, dc) in list(zip(outgoing, exchange_steps(n_seq)))[1:]:
            route = [(i, (i // CORES + dz) % n_z * CORES + (i + dc) % CORES) for i in range(n_seq)]
            arrived.append(lax.ppermute(part, "seq", route))
    else:
        arrived = [
            lax.all_to_all(
                outgoing[0].reshape(n_seq, chunk, width), "seq", split_axis=0, concat_axis=0, tiled=True
            ).reshape(sent, width)
        ]
    placed = pl.pallas_call(
        place_kernel,
        out_shape=rows_of(row_total, GROUP * width),
        in_specs=[vmem] * (1 + pieces),
        out_specs=pl.BlockSpec(memory_space=pltpu.HBM),
        scratch_shapes=[pltpu.VMEM((row_total, GROUP * width), jnp.bfloat16), pltpu.SemaphoreType.DMA((GROUP,))],
        compiler_params=small,
    )(place, *arrived)
    return placed[None]


def solution(mesh):
    placed = (
        P("enc", "seq", None),
        P("enc", "seq", None),
        P("enc", "seq"),
        P("enc", "seq"),
        P("enc", "seq"),
        P("enc", "seq"),
        P(),
        P(),
        P(),
    )
    return jax.shard_map(
        per_device, mesh=mesh, in_specs=placed, out_specs=P("enc", "seq", None), check_vma=False
    )
```

profile of v0, /device:TPU:0, one launch (start us, length us, event | category | flops | bytes accessed | tf_op | source)
XLA Modules:
  0.0 26.6 jit_solution(14736734193783043598)
XLA Ops:
  0.0 0.0 copy-start.1
  0.0 0.0 copy-start
  0.7 3.2 %shard_map.92 = bf16[64,1280]{1,0:T(8,128)(2,1)S(1)} custom-call(s32[1,1]{1,0:T(1,128)S(6)} %copy.10.count_ref, bf16[4,64,3840]{2,1,0:T(8,128)(2,1)} %qkv_hbm.3, bf16[4,64,1280]{2,1,0:T(8,128)(2,1)} %resid_hbm.3, bf16[1280,1280]{1,0:T(8,128)(2,1)} %weight_hbm.3, bf16[1280]{0:T(1024)(128)(2,1)} %bias_hbm.3, bf16[1280]{0:T(1024)(128)(2,1)} %gain_hbm.3), custom_call_target="tpu_custom_call" | custom-call | flops 251658240 | bytes 4096000 | tf_op jit(solution)/shard_map/pallas_call | solution.py:194
  3.9 3.0 %collective-permute-start = (bf16[64,1280]{1,0:T(8,128)(2,1)S(1)}, bf16[64,1280]{1,0:T(8,128)(2,1)S(1)}, u32[]{:S(2)}, u32[]{:S(2)}) collective-permute-start(bf16[64,1280]{1,0:T(8,128)(2,1)S(1)} %shard_map.92), channel_id=1, source_target_pairs={{24,0},{0,8},{8,16},{16,24},{25,1},{1,9},{9,17},{17,25},{26,2},{2,... | collective-permute-start | bytes 491528 | tf_op jit(solution)/shard_map/ppermute | solution.py:284
  7.6 0.0 copy-done.1
  7.6 0.0 copy-done
  7.6 4.3 %shard_map.91 = (bf16[192,1280]{1,0:T(8,128)(2,1)S(1)}, bf16[192,64]{1,0:T(8,128)(2,1)S(1)}, bf16[192,192]{1,0:T(8,128)(2,1)S(1)}) custom-call(s32[1,1]{1,0:T(1,128)S(6)} %copy.10.count_ref, s32[1,1]{1,0:T(1,128)S(6)} %copy.11.send_ref, s32[1,1]{1,0:T(1,128)} %bitcast.me_ref, s32[1,48]{1,0:T(1,128)S(1)} %copy-done, s32[1,48]{1,0:T(1,128)S(1)} %copy-done.1, ...), custom_call_target="tpu_custom_call" | custom-call | flops 754974720 | bytes 5734400 | tf_op jit(solution)/shard_map/pallas_call | solution.py:194
  11.9 0.2 collective-permute-done.borrowed_ref
  12.1 0.3 %shard_map.93 = (bf16[24,1280]{1,0:T(8,128)(2,1)S(1)}, bf16[24,1280]{1,0:T(8,128)(2,1)S(1)}, bf16[24,1280]{1,0:T(8,128)(2,1)S(1)}, bf16[24,1280]{1,0:T(8,128)(2,...) custom-call(bf16[192,1280]{1,0:T(8,128)(2,1)S(1)} %get-tuple-element, ...), custom_call_target="tpu_custom_call" | custom-call | tf_op jit(solution)/shard_map/pallas_call | solution.py:296
  12.3 2.8 %collective-permute-start.1 = (bf16[24,1280]{1,0:T(8,128)(2,1)S(1)}, bf16[24,1280]{1,0:T(8,128)(2,1)S(1)}, u32[]{:S(2)}, u32[]{:S(2)}) collective-permute-start(bf16[24,1280]{1,0:T(8,128)(2,1)S(1)} %get-tuple-element.20), channel_id=1, source_target_pairs={{0,4},{1,5},{2,6},{3,7},{4,0},{5,1},{6,2},{7,3},{8,12},{9,13},{10,... | collective-permute-start | bytes 184328 | tf_op jit(solution)/shard_map/ppermute | solution.py:309
  15.2 0.0 collective-permute-start.2
  15.2 1.6 %collective-permute-start.3 = (bf16[24,1280]{1,0:T(8,128)(2,1)S(1)}, bf16[24,1280]{1,0:T(8,128)(2,1)S(1)}, u32[]{:S(2)}, u32[]{:S(2)}) collective-permute-start(bf16[24,1280]{1,0:T(8,128)(2,1)S(1)} %get-tuple-element.22), channel_id=1, source_target_pairs={{0,2},{1,3},{2,4},{3,5},{4,6},{5,7},{6,0},{7,1},{8,10},{9,11},{10,... | collective-permute-start | bytes 184328 | tf_op jit(solution)/shard_map/ppermute | solution.py:309
  16.8 2.2 %collective-permute-start.4 = (bf16[24,1280]{1,0:T(8,128)(2,1)S(1)}, bf16[24,1280]{1,0:T(8,128)(2,1)S(1)}, u32[]{:S(2)}, u32[]{:S(2)}) collective-permute-start(bf16[24,1280]{1,0:T(8,128)(2,1)S(1)} %get-tuple-element.23), channel_id=1, source_target_pairs={{0,6},{1,7},{2,0},{3,1},{4,2},{5,3},{6,4},{7,5},{8,14},{9,15},{10,... | collective-permute-start | bytes 184328 | tf_op jit(solution)/shard_map/ppermute | solution.py:309
  19.0 0.0 collective-permute-start.5
  19.0 0.0 collective-permute-done.1.refs_1_
  19.0 3.5 %collective-permute-start.6 = (bf16[24,1280]{1,0:T(8,128)(2,1)S(1)}, bf16[24,1280]{1,0:T(8,128)(2,1)S(1)}, u32[]{:S(2)}, u32[]{:S(2)}) collective-permute-start(bf16[24,1280]{1,0:T(8,128)(2,1)S(1)} %get-tuple-element.25), channel_id=1, source_target_pairs={{0,7},{1,6},{2,1},{3,0},{4,3},{5,2},{6,5},{7,4},{8,15},{9,14},{10,... | collective-permute-start | bytes 184328 | tf_op jit(solution)/shard_map/ppermute | solution.py:309
  22.5 0.5 %collective-permute-done.2.refs_2_ = bf16[24,1280]{1,0:T(8,128)(2,1)S(1)} collective-permute-done((bf16[24,1280]{1,0:T(8,128)(2,1)S(1)}, bf16[24,1280]{1,0:T(8,128)(2,1)S(1)}, u32[]{:S(2)}, u32[]{:S(2)}) %collective-permute-start.2) | collective-permute-done | bytes 61472 | tf_op jit(solution)/shard_map/ppermute | solution.py:309
  23.0 0.6 %collective-permute-start.7 = (bf16[24,1280]{1,0:T(8,128)(2,1)S(1)}, bf16[24,1280]{1,0:T(8,128)(2,1)S(1)}, u32[]{:S(2)}, u32[]{:S(2)}) collective-permute-start(bf16[24,1280]{1,0:T(8,128)(2,1)S(1)} %get-tuple-element.26), channel_id=1, source_target_pairs={{0,1},{1,0},{2,3},{3,2},{4,5},{5,4},{6,7},{7,6},{8,9},{9,8},{10,11... | collective-permute-start | bytes 184328 | tf_op jit(solution)/shard_map/ppermute | solution.py:309
  23.6 0.0 collective-permute-done.3.refs_3_
  23.6 0.0 collective-permute-done.4.refs_4_
  23.6 1.5 %collective-permute-done.5.refs_5_ = bf16[24,1280]{1,0:T(8,128)(2,1)S(1)} collective-permute-done((bf16[24,1280]{1,0:T(8,128)(2,1)S(1)}, bf16[24,1280]{1,0:T(8,128)(2,1)S(1)}, u32[]{:S(2)}, u32[]{:S(2)}) %collective-permute-start.5) | collective-permute-done | bytes 61472 | tf_op jit(solution)/shard_map/ppermute | solution.py:309
  25.1 0.3 %collective-permute-done.6.refs_6_ = bf16[24,1280]{1,0:T(8,128)(2,1)S(1)} collective-permute-done((bf16[24,1280]{1,0:T(8,128)(2,1)S(1)}, bf16[24,1280]{1,0:T(8,128)(2,1)S(1)}, u32[]{:S(2)}, u32[]{:S(2)}) %collective-permute-start.6) | collective-permute-done | bytes 61472 | tf_op jit(solution)/shard_map/ppermute | solution.py:309
  25.4 0.0 collective-permute-done.7.refs_7_
  25.4 1.2 %shard_map.94 = bf16[48,5120]{1,0:T(8,128)(2,1)} custom-call(bf16[192,192]{1,0:T(8,128)(2,1)S(1)} %get-tuple-element.16.place_ref, bf16[24,1280]{1,0:T(8,128)(2,1)S(1)} %get-tuple-element.19.refs_0_, bf16[24,1280]{1,0:T(8,128)(2,1)S(1)} %collective-permute-done.1.refs_1_, bf16[24,1280]{1,0:T(8,128)(2,1)S(1)} %collective-permute-done.2.refs_2_, ...), custom_call_target="tpu_custom_call" | custom-call | tf_op jit(solution)/shard_map/pallas_call | solution.py:316
Async XLA Ops:
  0.0 7.6 %copy-start.1 = (s32[1,48]{1,0:T(1,128)S(1)}, s32[1,48]{1,0:T(1,128)}, u32[]{:S(2)}) copy-start(s32[1,48]{1,0:T(1,128)} %row_ref.1) | copy-start | bytes 580
  0.0 7.6 %copy-start = (s32[1,48]{1,0:T(1,128)S(1)}, s32[1,48]{1,0:T(1,128)}, u32[]{:S(2)}) copy-start(s32[1,48]{1,0:T(1,128)} %slot_ref.1) | copy-start | bytes 580
  3.9 8.1 %collective-permute-start = (bf16[64,1280]{1,0:T(8,128)(2,1)S(1)}, bf16[64,1280]{1,0:T(8,128)(2,1)S(1)}, u32[]{:S(2)}, u32[]{:S(2)}) collective-permute-start(bf16[64,1280]{1,0:T(8,128)(2,1)S(1)} %shard_map.92), channel_id=1, source_target_pairs={{24,0},{0,8},{8,16},{16,24},{25,1},{1,9},{9,17},{17,25},{26,2},{2,... | collective-permute-start | bytes 491528 | tf_op jit(solution)/shard_map/ppermute | solution.py:284
  12.3 6.7 %collective-permute-start.1 = (bf16[24,1280]{1,0:T(8,128)(2,1)S(1)}, bf16[24,1280]{1,0:T(8,128)(2,1)S(1)}, u32[]{:S(2)}, u32[]{:S(2)}) collective-permute-start(bf16[24,1280]{1,0:T(8,128)(2,1)S(1)} %get-tuple-element.20), channel_id=1, source_target_pairs={{0,4},{1,5},{2,6},{3,7},{4,0},{5,1},{6,2},{7,3},{8,12},{9,13},{10,... | collective-permute-start | bytes 184328 | tf_op jit(solution)/shard_map/ppermute | solution.py:309
  15.2 7.8 %collective-permute-start.2 = (bf16[24,1280]{1,0:T(8,128)(2,1)S(1)}, bf16[24,1280]{1,0:T(8,128)(2,1)S(1)}, u32[]{:S(2)}, u32[]{:S(2)}) collective-permute-start(bf16[24,1280]{1,0:T(8,128)(2,1)S(1)} %get-tuple-element.21), channel_id=1, source_target_pairs={{0,5},{1,4},{2,7},{3,6},{4,1},{5,0},{6,3},{7,2},{8,13},{9,12},{10,... | collective-permute-start | bytes 184328 | tf_op jit(solution)/shard_map/ppermute | solution.py:309
  15.2 8.4 %collective-permute-start.3 = (bf16[24,1280]{1,0:T(8,128)(2,1)S(1)}, bf16[24,1280]{1,0:T(8,128)(2,1)S(1)}, u32[]{:S(2)}, u32[]{:S(2)}) collective-permute-start(bf16[24,1280]{1,0:T(8,128)(2,1)S(1)} %get-tuple-element.22), channel_id=1, source_target_pairs={{0,2},{1,3},{2,4},{3,5},{4,6},{5,7},{6,0},{7,1},{8,10},{9,11},{10,... | collective-permute-start | bytes 184328 | tf_op jit(solution)/shard_map/ppermute | solution.py:309
  16.8 6.9 %collective-permute-start.4 = (bf16[24,1280]{1,0:T(8,128)(2,1)S(1)}, bf16[24,1280]{1,0:T(8,128)(2,1)S(1)}, u32[]{:S(2)}, u32[]{:S(2)}) collective-permute-start(bf16[24,1280]{1,0:T(8,128)(2,1)S(1)} %get-tuple-element.23), channel_id=1, source_target_pairs={{0,6},{1,7},{2,0},{3,1},{4,2},{5,3},{6,4},{7,5},{8,14},{9,15},{10,... | collective-permute-start | bytes 184328 | tf_op jit(solution)/shard_map/ppermute | solution.py:309
  19.0 6.1 %collective-permute-start.5 = (bf16[24,1280]{1,0:T(8,128)(2,1)S(1)}, bf16[24,1280]{1,0:T(8,128)(2,1)S(1)}, u32[]{:S(2)}, u32[]{:S(2)}) collective-permute-start(bf16[24,1280]{1,0:T(8,128)(2,1)S(1)} %get-tuple-element.24), channel_id=1, source_target_pairs={{0,3},{1,2},{2,5},{3,4},{4,7},{5,6},{6,1},{7,0},{8,11},{9,10},{10,... | collective-permute-start | bytes 184328 | tf_op jit(solution)/shard_map/ppermute | solution.py:309
  19.0 6.4 %collective-permute-start.6 = (bf16[24,1280]{1,0:T(8,128)(2,1)S(1)}, bf16[24,1280]{1,0:T(8,128)(2,1)S(1)}, u32[]{:S(2)}, u32[]{:S(2)}) collective-permute-start(bf16[24,1280]{1,0:T(8,128)(2,1)S(1)} %get-tuple-element.25), channel_id=1, source_target_pairs={{0,7},{1,6},{2,1},{3,0},{4,3},{5,2},{6,5},{7,4},{8,15},{9,14},{10,... | collective-permute-start | bytes 184328 | tf_op jit(solution)/shard_map/ppermute | solution.py:309
  23.0 2.4 %collective-permute-start.7 = (bf16[24,1280]{1,0:T(8,128)(2,1)S(1)}, bf16[24,1280]{1,0:T(8,128)(2,1)S(1)}, u32[]{:S(2)}, u32[]{:S(2)}) collective-permute-start(bf16[24,1280]{1,0:T(8,128)(2,1)S(1)} %get-tuple-element.26), channel_id=1, source_target_pairs={{0,1},{1,0},{2,3},{3,2},{4,5},{5,4},{6,7},{7,6},{8,9},{9,8},{10,11... | collective-permute-start | bytes 184328 | tf_op jit(solution)/shard_map/ppermute | solution.py:309
where the time goes:
time: 26.7 us; the launch traced here: 26.6 us
  starting transfers between devices  13.8 us (52%)
  Pallas kernels  8.94 us (33%)
  waiting for transfers between devices  2.43 us (9%)
  between operations  1.38 us (5%)
    ppermute x7, starting transfers between devices, per_device(): arrived.append(lax.ppermute(part, 'seq', route))  10.8 us
    pallas_call x2, Pallas kernels, encode_call(): pl.pallas_call(kernel, out_shape=out_shape, in_specs=[smem] * len(scalars...  7.52 us
    ppermute x1, starting transfers between devices, per_device(): lax.ppermute(lent, 'enc', [((i - 1) % n_enc, i) for i in range(n_enc)])  2.99 us
    ppermute x7, waiting for transfers between devices, per_device(): arrived.append(lax.ppermute(part, 'seq', route))  2.25 us
    pallas_call x1, Pallas kernels, per_device(): pl.pallas_call(place_kernel, out_shape=rows_of(row_total, GROUP * width),...  1.16 us
  transfers between devices with their start and end apart: 8, of which 4 were waited for; matrix products, arithmetic and copies ran while one was open for 0% of the time, Pallas kernels for 16%

commit v1 on v0

--- a/solution.py
+++ b/solution.py
@@ -26,47 +26,56 @@
     return match.astype(jnp.float32).astype(jnp.bfloat16)
 
 
-def attend(q, k, v, out_ref, row0, width):
+def head_pairs(width):
     head = width // HEADS
-    rate = 1.0 / math.sqrt(head)
+    spans = []
+    for start in range(0, width, 2 * head):
+        lo = start // LANES * LANES
+        spans.append((start, lo, -(-(start + 2 * head) // LANES) * LANES))
+    return spans
+
+
+def mask_period(width):
+    return LANES // math.gcd(LANES, 2 * (width // HEADS))
+
+
+def mask_scratch(width):
+    return pltpu.VMEM((mask_period(width), 2 * WIN, 2 * LANES), jnp.bfloat16)
+
+
+def make_masks(masks, width):
+    head = width // HEADS
+    for i in range(masks.shape[0]):
+        start, lo, hi = head_pairs(width)[i]
+        column = lax.broadcasted_iota(jnp.int32, masks.shape[1:], 1) + lo
+        row = lax.broadcasted_iota(jnp.int32, masks.shape[1:], 0)
+        begin = jnp.where(row < WIN, start, start + head)
+        masks[i] = one_hot((column >= begin) & (column < begin + head))
+
+
+def attend(qkv, b, masks, out_ref, width):
+    rate = math.log2(math.e) / math.sqrt(width // HEADS)
     totals = [None] * (width // LANES)
-    sums = [None] * (width // LANES)
-    first_half = lax.broadcasted_iota(jnp.int32, (WIN, 2 * WIN), 1) < WIN
-    for pair in range(HEADS // 2):
-        start = 2 * pair * head
-        lo = start // LANES * LANES
-        hi = -(-(start + 2 * head) // LANES) * LANES
-        column = lax.broadcasted_iota(jnp.int32, (2 * WIN, hi - lo), 1) + lo
-        row = lax.broadcasted_iota(jnp.int32, (2 * WIN, hi - lo), 0)
-        begin = jnp.where(row < WIN, start, start + head)
-        mask = one_hot((column >= begin) & (column < begin + head))
-        kw, vw = k(lo, hi), v(lo, hi)
+    first = lax.broadcasted_iota(jnp.int32, (WIN, 2 * WIN), 1) < WIN
+    for pair, (_, lo, hi) in enumerate(head_pairs(width)):
+        mask = masks[pair % masks.shape[0]]
+        kw = qkv[b, :, width + lo : width + hi]
+        vw = qkv[b, :, 2 * width + lo : 2 * width + hi]
         keys = jnp.concatenate([kw, kw], axis=0) * mask
         values = jnp.concatenate([vw, vw], axis=0) * mask
-        scores = lax.dot_general(q(lo, hi), keys, NT, preferred_element_type=jnp.float32)
-        top0 = jnp.max(jnp.where(first_half, scores, -jnp.inf), axis=1, keepdims=True)
-        top1 = jnp.max(jnp.where(first_half, -jnp.inf, scores), axis=1, keepdims=True)
-        raised = jnp.exp((scores - jnp.where(first_half, top0, top1)) * rate).astype(jnp.bfloat16)
-        part = dot32(raised, values)
-        norm = dot32(raised, mask)
+        scores = lax.dot_general(qkv[b, :, lo:hi], keys, NT, preferred_element_type=jnp.float32)
+        top0 = jnp.max(jnp.where(first, scores, -jnp.inf), axis=1, keepdims=True)
+        top1 = jnp.max(jnp.where(first, -jnp.inf, scores), axis=1, keepdims=True)
+        raised = jnp.exp2((scores - jnp.where(first, top0, top1)) * rate)
+        sum0 = jnp.sum(jnp.where(first, raised, 0.0), axis=1, keepdims=True)
+        sum1 = jnp.sum(jnp.where(first, 0.0, raised), axis=1, keepdims=True)
+        probs = (raised * jnp.where(first, 1.0 / sum0, 1.0 / sum1)).astype(jnp.bfloat16)
+        part = dot32(probs, values)
         for tile in range(lo // LANES, hi // LANES):
-            at = slice(tile * LANES - lo, (tile + 1) * LANES - lo)
-            totals[tile] = part[:, at] if totals[tile] is None else totals[tile] + part[:, at]
-            sums[tile] = norm[:, at] if sums[tile] is None else sums[tile] + norm[:, at]
-    for tile in range(width // LANES):
-        out_ref[row0 : row0 + WIN, tile * LANES : (tile + 1) * LANES] = (totals[tile] / sums[tile]).astype(
-            jnp.bfloat16
-        )
-
-
-def attend_all(qkv, attended, width):
-    for b in range(qkv.shape[0]):
-        attend(
-            lambda lo, hi, b=b: qkv[b, :, lo:hi],
-            lambda lo, hi, b=b: qkv[b, :, width + lo : width + hi],
-            lambda lo, hi, b=b: qkv[b, :, 2 * width + lo : 2 * width + hi],
-            attended, b * WIN, width,
-        )
+            piece = part[:, tile * LANES - lo : (tile + 1) * LANES - lo]
+            totals[tile] = piece if totals[tile] is None else totals[tile] + piece
+    for tile, total in enumerate(totals):
+        out_ref[b * WIN : (b + 1) * WIN, tile * LANES : (tile + 1) * LANES] = total.astype(jnp.bfloat16)
 
 
 def project(attended, resid, weight, bias, gain, hidden, out_ref):
@@ -87,23 +96,25 @@
 
 def lent_kernel(
     count_ref, qkv_hbm, resid_hbm, weight_hbm, bias_hbm, gain_hbm, out_ref,
-    qkv, resid, weight, attended, hidden, bias, gain, sems, weight_sems,
+    qkv, resid, weight, attended, hidden, bias, gain, masks, sems, weight_sems,
 ):
     width = resid.shape[2]
     at = pl.ds(count_ref[0, 0] - 1, 1)
-    step = width // weight_sems.shape[0]
+    step = 2 * LANES
     chunks = [slice(lo, lo + step) for lo in range(0, width, step)]
+    parts = [slice(lo, min(lo + 2 * step, width)) for lo in range(0, width, 2 * step)]
     qkv_copy = pltpu.make_async_copy(qkv_hbm.at[at], qkv, sems.at[0])
     weight_copies = [
-        pltpu.make_async_copy(weight_hbm.at[part], weight.at[part], weight_sems.at[i]) for i, part in enumerate(chunks)
+        pltpu.make_async_copy(weight_hbm.at[part], weight.at[part], weight_sems.at[i]) for i, part in enumerate(parts)
     ]
     pairs = [(resid_hbm.at[at], resid), (bias_hbm, bias), (gain_hbm, gain)]
     other_copies = [pltpu.make_async_copy(a, b, sems.at[i + 1]) for i, (a, b) in enumerate(pairs)]
     for copy in [qkv_copy] + weight_copies[:-1] + other_copies + weight_copies[-1:]:
         copy.start()
+    make_masks(masks, width)
     qkv_copy.wait()
-    attend_all(qkv, attended, width)
-    for copy, part in list(zip(weight_copies, chunks))[:-1]:
+    attend(qkv, 0, masks, attended, width)
+    for copy, part in list(zip(weight_copies, parts))[:-1]:
         copy.wait()
         for cols in chunks:
             h = dot32(attended[:, part], weight[part, cols])
@@ -116,7 +127,7 @@
     weight_copies[-1].wait()
     squares = jnp.zeros((WIN, 1), jnp.float32)
     for cols in chunks:
-        h = hidden[:, cols] + dot32(attended[:, chunks[-1]], weight[chunks[-1], cols])
+        h = hidden[:, cols] + dot32(attended[:, parts[-1]], weight[parts[-1], cols])
         hidden[:, cols] = h
         squares = squares + jnp.sum(h * h, axis=1, keepdims=True)
     scale = lax.rsqrt(squares * (1.0 / width) + EPS)
@@ -124,14 +135,17 @@
         out_ref[:, cols] = (hidden[:, cols] * scale * gain[cols].astype(jnp.float32).reshape(1, step)).astype(jnp.bfloat16)
 
 
-def encode(qkv_hbm, resid_hbm, weight_hbm, bias_hbm, gain_hbm, out_ref, qkv, resid, weight, attended, hidden, bias, gain, sems):
+def encode(qkv_hbm, resid_hbm, weight_hbm, bias_hbm, gain_hbm, out_ref, qkv, resid, weight, attended, hidden, bias, gain, masks, sems):
     at = pl.ds(0, qkv.shape[0])
     pairs = [(qkv_hbm.at[at], qkv), (weight_hbm, weight), (resid_hbm.at[at], resid), (bias_hbm, bias), (gain_hbm, gain)]
     copies = [pltpu.make_async_copy(a, b, sems.at[i]) for i, (a, b) in enumerate(pairs)]
     for copy in copies:
         copy.start()
+    width = resid.shape[2]
+    make_masks(masks, width)
     copies[0].wait()
-    attend_all(qkv, attended, resid.shape[2])
+    for b in range(qkv.shape[0]):
+        attend(qkv, b, masks, attended, width)
     for copy in copies[1:]:
         copy.wait()
     project(attended, resid, weight, bias, gain, hidden, out_ref)
@@ -205,6 +219,7 @@
             pltpu.VMEM((rows, width), jnp.float32),
             pltpu.VMEM((width,), jnp.bfloat16),
             pltpu.VMEM((width,), jnp.bfloat16),
+            mask_scratch(width),
             pltpu.SemaphoreType.DMA((5,)),
             *after,
         ],
@@ -279,7 +294,7 @@
         return jax.ShapeDtypeStruct((count, columns), jnp.bfloat16)
 
     data = (qkv, resid, out_weight, out_bias, norm_gain)
-    weight_parts = [pltpu.SemaphoreType.DMA((width // (2 * LANES),))]
+    weight_parts = [pltpu.SemaphoreType.DMA((-(-width // (4 * LANES)),))]
     lent = encode_call(lent_kernel, 1, [block_count], [], *data, rows_of(WIN), after=weight_parts)
     borrowed = lax.ppermute(lent, "enc", [((i - 1) % n_enc, i) for i in range(n_enc)])
 

time: 26.7 us -> 34.5 us (1.29)
  Pallas kernels: 8.94 us -> 16.9 us
  waiting for transfers between devices: 2.43 us -> 1.36 us
  starting transfers between devices: 13.8 us -> 14.7 us
    pallas_call x2, Pallas kernels: 7.52 us -> 15.5 us  [encode_call(): pl.pallas_call(kernel, out_shape=out_shape, in_specs=[smem] * len(scalars...]
    ppermute x7, starting transfers between devices: 10.8 us -> 11.7 us  [per_device(): arrived.append(lax.ppermute(part, 'seq', route))]
    ppermute x7, waiting for transfers between devices: 2.25 us -> 1.36 us  [per_device(): arrived.append(lax.ppermute(part, 'seq', route))]
  transfers between devices with their start and end apart: 8 -> 8, of which waited for: 4 -> 3; matrix products, arithmetic and copies ran while one was open for 0% -> 0% of each run, Pallas kernels for 16% -> 31%
where the time goes in v1:
time: 34.5 us; the launch traced here: 34.4 us
  Pallas kernels  16.9 us (49%)
  starting transfers between devices  14.7 us (43%)
  between operations  1.39 us (4%)
  waiting for transfers between devices  1.36 us (4%)
    pallas_call x2, Pallas kernels, encode_call(): pl.pallas_call(kernel, out_shape=out_shape, in_specs=[smem] * len(scalars...  15.5 us
    ppermute x7, starting transfers between devices, per_device(): arrived.append(lax.ppermute(part, 'seq', route))  11.7 us
    ppermute x1, starting transfers between devices, per_device(): lax.ppermute(lent, 'enc', [((i - 1) % n_enc, i) for i in range(n_enc)])  2.99 us
    ppermute x7, waiting for transfers between devices, per_device(): arrived.append(lax.ppermute(part, 'seq', route))  1.36 us
    pallas_call x1, Pallas kernels, per_device(): pl.pallas_call(place_kernel, out_shape=rows_of(row_total, GROUP * width),...  1.15 us
  transfers between devices with their start and end apart: 8, of which 3 were waited for; matrix products, arithmetic and copies ran while one was open for 0% of the time, Pallas kernels for 31%

profile of v1, /device:TPU:0, one launch (start us, length us, event | category | flops | bytes accessed | tf_op | source)
XLA Modules:
  0.0 34.4 jit_solution(5156068972010041923)
XLA Ops:
  0.0 0.0 copy-start.1
  0.0 0.0 copy-start
  0.7 4.7 %shard_map.92 = bf16[64,1280]{1,0:T(8,128)(2,1)S(1)} custom-call(s32[1,1]{1,0:T(1,128)S(6)} %copy.10.count_ref, bf16[4,64,3840]{2,1,0:T(8,128)(2,1)} %qkv_hbm.3, bf16[4,64,1280]{2,1,0:T(8,128)(2,1)} %resid_hbm.3, bf16[1280,1280]{1,0:T(8,128)(2,1)} %weight_hbm.3, bf16[1280]{0:T(1024)(128)(2,1)} %bias_hbm.3, bf16[1280]{0:T(1024)(128)(2,1)} %gain_hbm.3), custom_call_target="tpu_custom_call" | custom-call | flops 251658240 | bytes 4096000 | tf_op jit(solution)/shard_map/pallas_call | solution.py:208
  5.4 3.0 %collective-permute-start = (bf16[64,1280]{1,0:T(8,128)(2,1)S(1)}, bf16[64,1280]{1,0:T(8,128)(2,1)S(1)}, u32[]{:S(2)}, u32[]{:S(2)}) collective-permute-start(bf16[64,1280]{1,0:T(8,128)(2,1)S(1)} %shard_map.92), channel_id=1, source_target_pairs={{24,0},{0,8},{8,16},{16,24},{25,1},{1,9},{9,17},{17,25},{26,2},{2,... | collective-permute-start | bytes 491528 | tf_op jit(solution)/shard_map/ppermute | solution.py:299
  9.0 0.0 copy-done.1
  9.0 0.0 copy-done
  9.0 10.8 %shard_map.91 = (bf16[192,1280]{1,0:T(8,128)(2,1)S(1)}, bf16[192,64]{1,0:T(8,128)(2,1)S(1)}, bf16[192,192]{1,0:T(8,128)(2,1)S(1)}) custom-call(s32[1,1]{1,0:T(1,128)S(6)} %copy.10.count_ref, s32[1,1]{1,0:T(1,128)S(6)} %copy.11.send_ref, s32[1,1]{1,0:T(1,128)} %bitcast.me_ref, s32[1,48]{1,0:T(1,128)S(1)} %copy-done, s32[1,48]{1,0:T(1,128)S(1)} %copy-done.1, ...), custom_call_target="tpu_custom_call" | custom-call | flops 754974720 | bytes 5734400 | tf_op jit(solution)/shard_map/pallas_call | solution.py:208
  19.9 0.0 collective-permute-done.borrowed_ref
  19.9 0.3 shard_map.93
  20.2 2.7 %collective-permute-start.1 = (bf16[24,1280]{1,0:T(8,128)(2,1)S(1)}, bf16[24,1280]{1,0:T(8,128)(2,1)S(1)}, u32[]{:S(2)}, u32[]{:S(2)}) collective-permute-start(bf16[24,1280]{1,0:T(8,128)(2,1)S(1)} %get-tuple-element.20), channel_id=1, source_target_pairs={{0,4},{1,5},{2,6},{3,7},{4,0},{5,1},{6,2},{7,3},{8,12},{9,13},{10,... | collective-permute-start | bytes 184328 | tf_op jit(solution)/shard_map/ppermute | solution.py:324
  22.8 0.0 collective-permute-start.2
  22.8 1.6 %collective-permute-start.3 = (bf16[24,1280]{1,0:T(8,128)(2,1)S(1)}, bf16[24,1280]{1,0:T(8,128)(2,1)S(1)}, u32[]{:S(2)}, u32[]{:S(2)}) collective-permute-start(bf16[24,1280]{1,0:T(8,128)(2,1)S(1)} %get-tuple-element.22), channel_id=1, source_target_pairs={{0,2},{1,3},{2,4},{3,5},{4,6},{5,7},{6,0},{7,1},{8,10},{9,11},{10,... | collective-permute-start | bytes 184328 | tf_op jit(solution)/shard_map/ppermute | solution.py:324
  24.4 2.2 %collective-permute-start.4 = (bf16[24,1280]{1,0:T(8,128)(2,1)S(1)}, bf16[24,1280]{1,0:T(8,128)(2,1)S(1)}, u32[]{:S(2)}, u32[]{:S(2)}) collective-permute-start(bf16[24,1280]{1,0:T(8,128)(2,1)S(1)} %get-tuple-element.23), channel_id=1, source_target_pairs={{0,6},{1,7},{2,0},{3,1},{4,2},{5,3},{6,4},{7,5},{8,14},{9,15},{10,... | collective-permute-start | bytes 184328 | tf_op jit(solution)/shard_map/ppermute | solution.py:324
  26.6 0.0 collective-permute-start.5
  26.6 0.0 collective-permute-done.1.refs_1_
  26.6 3.5 %collective-permute-start.6 = (bf16[24,1280]{1,0:T(8,128)(2,1)S(1)}, bf16[24,1280]{1,0:T(8,128)(2,1)S(1)}, u32[]{:S(2)}, u32[]{:S(2)}) collective-permute-start(bf16[24,1280]{1,0:T(8,128)(2,1)S(1)} %get-tuple-element.25), channel_id=1, source_target_pairs={{0,7},{1,6},{2,1},{3,0},{4,3},{5,2},{6,5},{7,4},{8,15},{9,14},{10,... | collective-permute-start | bytes 184328 | tf_op jit(solution)/shard_map/ppermute | solution.py:324
  30.2 0.5 %collective-permute-done.2.refs_2_ = bf16[24,1280]{1,0:T(8,128)(2,1)S(1)} collective-permute-done((bf16[24,1280]{1,0:T(8,128)(2,1)S(1)}, bf16[24,1280]{1,0:T(8,128)(2,1)S(1)}, u32[]{:S(2)}, u32[]{:S(2)}) %collective-permute-start.2) | collective-permute-done | bytes 61472 | tf_op jit(solution)/shard_map/ppermute | solution.py:324
  30.6 1.7 %collective-permute-start.7 = (bf16[24,1280]{1,0:T(8,128)(2,1)S(1)}, bf16[24,1280]{1,0:T(8,128)(2,1)S(1)}, u32[]{:S(2)}, u32[]{:S(2)}) collective-permute-start(bf16[24,1280]{1,0:T(8,128)(2,1)S(1)} %get-tuple-element.26), channel_id=1, source_target_pairs={{0,1},{1,0},{2,3},{3,2},{4,5},{5,4},{6,7},{7,6},{8,9},{9,8},{10,11... | collective-permute-start | bytes 184328 | tf_op jit(solution)/shard_map/ppermute | solution.py:324
  32.3 0.0 collective-permute-done.3.refs_3_
  32.3 0.0 collective-permute-done.4.refs_4_
  32.3 0.4 %collective-permute-done.5.refs_5_ = bf16[24,1280]{1,0:T(8,128)(2,1)S(1)} collective-permute-done((bf16[24,1280]{1,0:T(8,128)(2,1)S(1)}, bf16[24,1280]{1,0:T(8,128)(2,1)S(1)}, u32[]{:S(2)}, u32[]{:S(2)}) %collective-permute-start.5) | collective-permute-done | bytes 61472 | tf_op jit(solution)/shard_map/ppermute | solution.py:324
  32.8 0.0 collective-permute-done.6.refs_6_
  32.8 0.5 %collective-permute-done.7.refs_7_ = bf16[24,1280]{1,0:T(8,128)(2,1)S(1)} collective-permute-done((bf16[24,1280]{1,0:T(8,128)(2,1)S(1)}, bf16[24,1280]{1,0:T(8,128)(2,1)S(1)}, u32[]{:S(2)}, u32[]{:S(2)}) %collective-permute-start.7) | collective-permute-done | bytes 61472 | tf_op jit(solution)/shard_map/ppermute | solution.py:324
  33.2 1.2 %shard_map.94 = bf16[48,5120]{1,0:T(8,128)(2,1)} custom-call(bf16[192,192]{1,0:T(8,128)(2,1)S(1)} %get-tuple-element.16.place_ref, bf16[24,1280]{1,0:T(8,128)(2,1)S(1)} %get-tuple-element.19.refs_0_, bf16[24,1280]{1,0:T(8,128)(2,1)S(1)} %collective-permute-done.1.refs_1_, bf16[24,1280]{1,0:T(8,128)(2,1)S(1)} %collective-permute-done.2.refs_2_, ...), custom_call_target="tpu_custom_call" | custom-call | tf_op jit(solution)/shard_map/pallas_call | solution.py:331
Async XLA Ops:
  0.0 9.0 %copy-start.1 = (s32[1,48]{1,0:T(1,128)S(1)}, s32[1,48]{1,0:T(1,128)}, u32[]{:S(2)}) copy-start(s32[1,48]{1,0:T(1,128)} %row_ref.1) | copy-start | bytes 580
  0.0 9.0 %copy-start = (s32[1,48]{1,0:T(1,128)S(1)}, s32[1,48]{1,0:T(1,128)}, u32[]{:S(2)}) copy-start(s32[1,48]{1,0:T(1,128)} %slot_ref.1) | copy-start | bytes 580
  5.4 14.5 %collective-permute-start = (bf16[64,1280]{1,0:T(8,128)(2,1)S(1)}, bf16[64,1280]{1,0:T(8,128)(2,1)S(1)}, u32[]{:S(2)}, u32[]{:S(2)}) collective-permute-start(bf16[64,1280]{1,0:T(8,128)(2,1)S(1)} %shard_map.92), channel_id=1, source_target_pairs={{24,0},{0,8},{8,16},{16,24},{25,1},{1,9},{9,17},{17,25},{26,2},{2,... | collective-permute-start | bytes 491528 | tf_op jit(solution)/shard_map/ppermute | solution.py:299
  20.2 6.5 %collective-permute-start.1 = (bf16[24,1280]{1,0:T(8,128)(2,1)S(1)}, bf16[24,1280]{1,0:T(8,128)(2,1)S(1)}, u32[]{:S(2)}, u32[]{:S(2)}) collective-permute-start(bf16[24,1280]{1,0:T(8,128)(2,1)S(1)} %get-tuple-element.20), channel_id=1, source_target_pairs={{0,4},{1,5},{2,6},{3,7},{4,0},{5,1},{6,2},{7,3},{8,12},{9,13},{10,... | collective-permute-start | bytes 184328 | tf_op jit(solution)/shard_map/ppermute | solution.py:324
  22.8 7.8 %collective-permute-start.2 = (bf16[24,1280]{1,0:T(8,128)(2,1)S(1)}, bf16[24,1280]{1,0:T(8,128)(2,1)S(1)}, u32[]{:S(2)}, u32[]{:S(2)}) collective-permute-start(bf16[24,1280]{1,0:T(8,128)(2,1)S(1)} %get-tuple-element.21), channel_id=1, source_target_pairs={{0,5},{1,4},{2,7},{3,6},{4,1},{5,0},{6,3},{7,2},{8,13},{9,12},{10,... | collective-permute-start | bytes 184328 | tf_op jit(solution)/shard_map/ppermute | solution.py:324
  22.8 9.5 %collective-permute-start.3 = (bf16[24,1280]{1,0:T(8,128)(2,1)S(1)}, bf16[24,1280]{1,0:T(8,128)(2,1)S(1)}, u32[]{:S(2)}, u32[]{:S(2)}) collective-permute-start(bf16[24,1280]{1,0:T(8,128)(2,1)S(1)} %get-tuple-element.22), channel_id=1, source_target_pairs={{0,2},{1,3},{2,4},{3,5},{4,6},{5,7},{6,0},{7,1},{8,10},{9,11},{10,... | collective-permute-start | bytes 184328 | tf_op jit(solution)/shard_map/ppermute | solution.py:324
  24.4 8.0 %collective-permute-start.4 = (bf16[24,1280]{1,0:T(8,128)(2,1)S(1)}, bf16[24,1280]{1,0:T(8,128)(2,1)S(1)}, u32[]{:S(2)}, u32[]{:S(2)}) collective-permute-start(bf16[24,1280]{1,0:T(8,128)(2,1)S(1)} %get-tuple-element.23), channel_id=1, source_target_pairs={{0,6},{1,7},{2,0},{3,1},{4,2},{5,3},{6,4},{7,5},{8,14},{9,15},{10,... | collective-permute-start | bytes 184328 | tf_op jit(solution)/shard_map/ppermute | solution.py:324
  26.6 6.1 %collective-permute-start.5 = (bf16[24,1280]{1,0:T(8,128)(2,1)S(1)}, bf16[24,1280]{1,0:T(8,128)(2,1)S(1)}, u32[]{:S(2)}, u32[]{:S(2)}) collective-permute-start(bf16[24,1280]{1,0:T(8,128)(2,1)S(1)} %get-tuple-element.24), channel_id=1, source_target_pairs={{0,3},{1,2},{2,5},{3,4},{4,7},{5,6},{6,1},{7,0},{8,11},{9,10},{10,... | collective-permute-start | bytes 184328 | tf_op jit(solution)/shard_map/ppermute | solution.py:324
  26.6 6.1 %collective-permute-start.6 = (bf16[24,1280]{1,0:T(8,128)(2,1)S(1)}, bf16[24,1280]{1,0:T(8,128)(2,1)S(1)}, u32[]{:S(2)}, u32[]{:S(2)}) collective-permute-start(bf16[24,1280]{1,0:T(8,128)(2,1)S(1)} %get-tuple-element.25), channel_id=1, source_target_pairs={{0,7},{1,6},{2,1},{3,0},{4,3},{5,2},{6,5},{7,4},{8,15},{9,14},{10,... | collective-permute-start | bytes 184328 | tf_op jit(solution)/shard_map/ppermute | solution.py:324
  30.6 2.6 %collective-permute-start.7 = (bf16[24,1280]{1,0:T(8,128)(2,1)S(1)}, bf16[24,1280]{1,0:T(8,128)(2,1)S(1)}, u32[]{:S(2)}, u32[]{:S(2)}) collective-permute-start(bf16[24,1280]{1,0:T(8,128)(2,1)S(1)} %get-tuple-element.26), channel_id=1, source_target_pairs={{0,1},{1,0},{2,3},{3,2},{4,5},{5,4},{6,7},{7,6},{8,9},{9,8},{10,11... | collective-permute-start | bytes 184328 | tf_op jit(solution)/shard_map/ppermute | solution.py:324

commit v2 on v0

--- a/solution.py
+++ b/solution.py
@@ -85,43 +85,19 @@
         out_ref[:, cols] = (hidden[:, cols] * scale * gain[cols].astype(jnp.float32).reshape(1, step)).astype(jnp.bfloat16)
 
 
-def lent_kernel(
-    count_ref, qkv_hbm, resid_hbm, weight_hbm, bias_hbm, gain_hbm, out_ref,
-    qkv, resid, weight, attended, hidden, bias, gain, sems, weight_sems,
-):
-    width = resid.shape[2]
+def lent_attention_kernel(count_ref, qkv_hbm, resid_hbm, attended, resid, qkv, sems):
     at = pl.ds(count_ref[0, 0] - 1, 1)
-    step = width // weight_sems.shape[0]
-    chunks = [slice(lo, lo + step) for lo in range(0, width, step)]
     qkv_copy = pltpu.make_async_copy(qkv_hbm.at[at], qkv, sems.at[0])
-    weight_copies = [
-        pltpu.make_async_copy(weight_hbm.at[part], weight.at[part], weight_sems.at[i]) for i, part in enumerate(chunks)
-    ]
-    pairs = [(resid_hbm.at[at], resid), (bias_hbm, bias), (gain_hbm, gain)]
-    other_copies = [pltpu.make_async_copy(a, b, sems.at[i + 1]) for i, (a, b) in enumerate(pairs)]
-    for copy in [qkv_copy] + weight_copies[:-1] + other_copies + weight_copies[-1:]:
-        copy.start()
+    resid_copy = pltpu.make_async_copy(resid_hbm.at[at], resid, sems.at[1])
+    qkv_copy.start()
+    resid_copy.start()
     qkv_copy.wait()
-    attend_all(qkv, attended, width)
-    for copy, part in list(zip(weight_copies, chunks))[:-1]:
-        copy.wait()
-        for cols in chunks:
-            h = dot32(attended[:, part], weight[part, cols])
-            hidden[:, cols] = h if part.start == 0 else hidden[:, cols] + h
-    for copy in other_copies:
-        copy.wait()
-    for cols in chunks:
-        h = hidden[:, cols] + bias[cols].astype(jnp.float32).reshape(1, step)
-        hidden[:, cols] = h + resid[0, :, cols].astype(jnp.float32)
-    weight_copies[-1].wait()
-    squares = jnp.zeros((WIN, 1), jnp.float32)
-    for cols in chunks:
-        h = hidden[:, cols] + dot32(attended[:, chunks[-1]], weight[chunks[-1], cols])
-        hidden[:, cols] = h
-        squares = squares + jnp.sum(h * h, axis=1, keepdims=True)
-    scale = lax.rsqrt(squares * (1.0 / width) + EPS)
-    for cols in chunks:
-        out_ref[:, cols] = (hidden[:, cols] * scale * gain[cols].astype(jnp.float32).reshape(1, step)).astype(jnp.bfloat16)
+    attend_all(qkv, attended, resid.shape[2])
+    resid_copy.wait()
+
+
+def lent_project_kernel(attended, resid, weight, bias, gain, out_ref, hidden):
+    project(attended, resid, weight, bias, gain, hidden, out_ref)
 
 
 def encode(qkv_hbm, resid_hbm, weight_hbm, bias_hbm, gain_hbm, out_ref, qkv, resid, weight, attended, hidden, bias, gain, sems):
@@ -185,7 +161,39 @@
     return [pltpu.with_memory_space_constraint(a, pltpu.HBM) for a in arrays]
 
 
-def encode_call(kernel, blocks, scalars, slots, qkv, resid, weight, bias, gain, out_shape, before=(), after=()):
+def encode_lent(count, qkv, resid, weight, bias, gain):
+    width = resid.shape[2]
+    vmem = pl.BlockSpec(memory_space=pltpu.VMEM)
+    hbm = pl.BlockSpec(memory_space=pltpu.HBM)
+    small = pltpu.CompilerParams(vmem_limit_bytes=16 << 20)
+    attended, rows = pl.pallas_call(
+        lent_attention_kernel,
+        out_shape=(
+            jax.ShapeDtypeStruct((WIN, width), jnp.bfloat16),
+            jax.ShapeDtypeStruct((1, WIN, width), jnp.bfloat16),
+        ),
+        in_specs=[pl.BlockSpec(memory_space=pltpu.SMEM), hbm, hbm],
+        out_specs=(vmem, vmem),
+        scratch_shapes=[pltpu.VMEM((1, WIN, 3 * width), jnp.bfloat16), pltpu.SemaphoreType.DMA((2,))],
+        compiler_params=small,
+        cost_estimate=pl.CostEstimate(
+            flops=8 << 30, bytes_accessed=16 << 20, transcendentals=WIN * WIN * HEADS
+        ),
+    )(count, *in_hbm(qkv, resid))
+    return pl.pallas_call(
+        lent_project_kernel,
+        out_shape=jax.ShapeDtypeStruct((WIN, width), jnp.bfloat16),
+        in_specs=[vmem] * 5,
+        out_specs=vmem,
+        scratch_shapes=[pltpu.VMEM((WIN, width), jnp.float32)],
+        compiler_params=small,
+        cost_estimate=pl.CostEstimate(
+            flops=2 * WIN * width * width, bytes_accessed=2 * (width * width + 3 * WIN * width), transcendentals=0
+        ),
+    )(attended, rows, weight, bias, gain)
+
+
+def encode_own(kernel, blocks, scalars, slots, qkv, resid, weight, bias, gain, out_shape, extra):
     width = resid.shape[2]
     rows = blocks * WIN
     vmem = pl.BlockSpec(memory_space=pltpu.VMEM)
@@ -196,8 +204,8 @@
         out_shape=out_shape,
         in_specs=[smem] * len(scalars) + [vmem] * len(slots) + [hbm] * 5,
         out_specs=jax.tree.map(lambda _: vmem, out_shape),
-        scratch_shapes=[
-            *before,
+        scratch_shapes=extra
+        + [
             pltpu.VMEM((blocks, WIN, 3 * width), jnp.bfloat16),
             pltpu.VMEM((blocks, WIN, width), jnp.bfloat16),
             pltpu.VMEM((width, width), jnp.bfloat16),
@@ -206,7 +214,6 @@
             pltpu.VMEM((width,), jnp.bfloat16),
             pltpu.VMEM((width,), jnp.bfloat16),
             pltpu.SemaphoreType.DMA((5,)),
-            *after,
         ],
         compiler_params=pltpu.CompilerParams(vmem_limit_bytes=24 << 20),
         cost_estimate=pl.CostEstimate(
@@ -279,14 +286,13 @@
         return jax.ShapeDtypeStruct((count, columns), jnp.bfloat16)
 
     data = (qkv, resid, out_weight, out_bias, norm_gain)
-    weight_parts = [pltpu.SemaphoreType.DMA((width // (2 * LANES),))]
-    lent = encode_call(lent_kernel, 1, [block_count], [], *data, rows_of(WIN), after=weight_parts)
+    lent = encode_lent(block_count, *data)
     borrowed = lax.ppermute(lent, "enc", [((i - 1) % n_enc, i) for i in range(n_enc)])
 
     by_steps = chunk % 8 == 0 and n_seq % CORES == 0
     peer = functools.partial(chip_peer, n_seq) if by_steps else lambda me, step, sign: step
     me = lax.axis_index("seq").astype(jnp.int32).reshape(1, 1)
-    packed, borrow, place = encode_call(
+    packed, borrow, place = encode_own(
         functools.partial(own_kernel, n_seq, cap, peer), blocks,
         [block_count, send_count, me], [send_slot, lm_row], *data,
         (rows_of(sent), rows_of(sent, WIN), rows_of(GROUP * row_total, sent)),

time: 26.7 us -> 26.4 us (0.989)
  Pallas kernels: 8.94 us -> 8.4 us
    pallas_call x2 -> x3, Pallas kernels: 7.52 us -> 6.98 us  [the longest x1 4.31 us: encode_own(): pl.pallas_call(kernel, out_shape=out_shape, in_specs=[smem] * len(scalars...]
where the time goes in v2:
time: 26.4 us; the launch traced here: 26.3 us
  starting transfers between devices  13.8 us (52%)
  Pallas kernels  8.4 us (32%)
  waiting for transfers between devices  2.42 us (9%)
  between operations  1.4 us (5%)
    ppermute x7, starting transfers between devices, per_device(): arrived.append(lax.ppermute(part, 'seq', route))  10.8 us
    pallas_call x1, Pallas kernels, encode_own(): pl.pallas_call(kernel, out_shape=out_shape, in_specs=[smem] * len(scalars...  4.31 us
    ppermute x1, starting transfers between devices, per_device(): lax.ppermute(lent, 'enc', [((i - 1) % n_enc, i) for i in range(n_enc)])  2.99 us
    ppermute x7, waiting for transfers between devices, per_device(): arrived.append(lax.ppermute(part, 'seq', route))  2.25 us
    pallas_call x1, Pallas kernels, encode_lent(): pl.pallas_call(lent_attention_kernel, out_shape=(jax.ShapeDtypeStruct((WI...  1.87 us
    pallas_call x1, Pallas kernels, per_device(): pl.pallas_call(place_kernel, out_shape=rows_of(row_total, GROUP * width),...  1.16 us
    pallas_call x1, Pallas kernels, encode_lent(): pl.pallas_call(lent_project_kernel, out_shape=jax.ShapeDtypeStruct((WIN,...  0.81 us
  transfers between devices with their start and end apart: 8, of which 4 were waited for; matrix products, arithmetic and copies ran while one was open for 0% of the time, Pallas kernels for 16%

profile of v2, /device:TPU:0, one launch (start us, length us, event | category | flops | bytes accessed | tf_op | source)
XLA Modules:
  0.0 26.3 jit_solution(2974557952719608333)
XLA Ops:
  0.7 0.0 copy-start
  0.7 0.0 copy-start.1
  0.7 0.0 copy-start.2
  0.7 1.9 %shard_map.92 = (bf16[64,1280]{1,0:T(8,128)(2,1)S(1)}, bf16[1,64,1280]{2,1,0:T(8,128)(2,1)S(1)}) custom-call(s32[1,1]{1,0:T(1,128)S(6)} %copy.10.count_ref, bf16[4,64,3840]{2,1,0:T(8,128)(2,1)} %qkv_hbm.3, bf16[4,64,1280]{2,1,0:T(8,128)(2,1)} %resid_hbm.3), custom_call_target="tpu_custom_call" | custom-call | flops 8589934592 | bytes 16777216 | tf_op jit(solution)/shard_map/pallas_call | solution.py:169
  2.6 0.0 copy-start.3
  2.6 0.0 copy-start.4
  2.6 0.2 copy-done
  2.8 0.0 copy-done.1
  2.8 0.0 copy-done.2
  2.8 0.8 %shard_map.93 = bf16[64,1280]{1,0:T(8,128)(2,1)S(1)} custom-call(bf16[64,1280]{1,0:T(8,128)(2,1)S(1)} %get-tuple-element.21.attended, bf16[1,64,1280]{2,1,0:T(8,128)(2,1)S(1)} %get-tuple-element.22.resid, bf16[1280,1280]{1,0:T(8,128)(2,1)S(1)} %copy-done, bf16[1280]{0:T(1024)(128)(2,1)S(1)} %copy-done.1, bf16[1280]{0:T(1024)(128)(2,1)S(1)} %copy-done.2), custom_call_target="tpu_custom_call" | custom-call | flops 209715200 | bytes 3768320 | tf_op jit(solution)/shard_map/pallas_call | solution.py:183
  3.6 3.0 %collective-permute-start = (bf16[64,1280]{1,0:T(8,128)(2,1)S(1)}, bf16[64,1280]{1,0:T(8,128)(2,1)S(1)}, u32[]{:S(2)}, u32[]{:S(2)}) collective-permute-start(bf16[64,1280]{1,0:T(8,128)(2,1)S(1)} %shard_map.93), channel_id=1, source_target_pairs={{24,0},{0,8},{8,16},{16,24},{25,1},{1,9},{9,17},{17,25},{26,2},{2,... | collective-permute-start | bytes 491528 | tf_op jit(solution)/shard_map/ppermute | solution.py:290
  7.3 0.0 copy-done.3
  7.3 0.0 copy-done.4
  7.3 4.3 %shard_map.91 = (bf16[192,1280]{1,0:T(8,128)(2,1)S(1)}, bf16[192,64]{1,0:T(8,128)(2,1)S(1)}, bf16[192,192]{1,0:T(8,128)(2,1)S(1)}) custom-call(s32[1,1]{1,0:T(1,128)S(6)} %copy.10.count_ref, s32[1,1]{1,0:T(1,128)S(6)} %copy.11.send_ref, s32[1,1]{1,0:T(1,128)} %bitcast.me_ref, s32[1,48]{1,0:T(1,128)S(1)} %copy-done.3, s32[1,48]{1,0:T(1,128)S(1)} %copy-done.4, ...), custom_call_target="tpu_custom_call" | custom-call | flops 754974720 | bytes 5734400 | tf_op jit(solution)/shard_map/pallas_call | solution.py:202
  11.6 0.2 collective-permute-done.borrowed_ref
  11.8 0.3 shard_map.94
  12.0 2.8 %collective-permute-start.1 = (bf16[24,1280]{1,0:T(8,128)(2,1)S(1)}, bf16[24,1280]{1,0:T(8,128)(2,1)S(1)}, u32[]{:S(2)}, u32[]{:S(2)}) collective-permute-start(bf16[24,1280]{1,0:T(8,128)(2,1)S(1)} %get-tuple-element.24), channel_id=1, source_target_pairs={{0,4},{1,5},{2,6},{3,7},{4,0},{5,1},{6,2},{7,3},{8,12},{9,13},{10,... | collective-permute-start | bytes 184328 | tf_op jit(solution)/shard_map/ppermute | solution.py:315
  14.9 0.0 collective-permute-start.2
  14.9 1.6 %collective-permute-start.3 = (bf16[24,1280]{1,0:T(8,128)(2,1)S(1)}, bf16[24,1280]{1,0:T(8,128)(2,1)S(1)}, u32[]{:S(2)}, u32[]{:S(2)}) collective-permute-start(bf16[24,1280]{1,0:T(8,128)(2,1)S(1)} %get-tuple-element.26), channel_id=1, source_target_pairs={{0,2},{1,3},{2,4},{3,5},{4,6},{5,7},{6,0},{7,1},{8,10},{9,11},{10,... | collective-permute-start | bytes 184328 | tf_op jit(solution)/shard_map/ppermute | solution.py:315
  16.5 2.2 %collective-permute-start.4 = (bf16[24,1280]{1,0:T(8,128)(2,1)S(1)}, bf16[24,1280]{1,0:T(8,128)(2,1)S(1)}, u32[]{:S(2)}, u32[]{:S(2)}) collective-permute-start(bf16[24,1280]{1,0:T(8,128)(2,1)S(1)} %get-tuple-element.27), channel_id=1, source_target_pairs={{0,6},{1,7},{2,0},{3,1},{4,2},{5,3},{6,4},{7,5},{8,14},{9,15},{10,... | collective-permute-start | bytes 184328 | tf_op jit(solution)/shard_map/ppermute | solution.py:315
  18.7 0.0 collective-permute-start.5
  18.7 0.0 collective-permute-done.1.refs_1_
  18.7 3.5 %collective-permute-start.6 = (bf16[24,1280]{1,0:T(8,128)(2,1)S(1)}, bf16[24,1280]{1,0:T(8,128)(2,1)S(1)}, u32[]{:S(2)}, u32[]{:S(2)}) collective-permute-start(bf16[24,1280]{1,0:T(8,128)(2,1)S(1)} %get-tuple-element.29), channel_id=1, source_target_pairs={{0,7},{1,6},{2,1},{3,0},{4,3},{5,2},{6,5},{7,4},{8,15},{9,14},{10,... | collective-permute-start | bytes 184328 | tf_op jit(solution)/shard_map/ppermute | solution.py:315
  22.3 0.5 %collective-permute-done.2.refs_2_ = bf16[24,1280]{1,0:T(8,128)(2,1)S(1)} collective-permute-done((bf16[24,1280]{1,0:T(8,128)(2,1)S(1)}, bf16[24,1280]{1,0:T(8,128)(2,1)S(1)}, u32[]{:S(2)}, u32[]{:S(2)}) %collective-permute-start.2) | collective-permute-done | bytes 61472 | tf_op jit(solution)/shard_map/ppermute | solution.py:315
  22.7 0.6 %collective-permute-start.7 = (bf16[24,1280]{1,0:T(8,128)(2,1)S(1)}, bf16[24,1280]{1,0:T(8,128)(2,1)S(1)}, u32[]{:S(2)}, u32[]{:S(2)}) collective-permute-start(bf16[24,1280]{1,0:T(8,128)(2,1)S(1)} %get-tuple-element.30), channel_id=1, source_target_pairs={{0,1},{1,0},{2,3},{3,2},{4,5},{5,4},{6,7},{7,6},{8,9},{9,8},{10,11... | collective-permute-start | bytes 184328 | tf_op jit(solution)/shard_map/ppermute | solution.py:315
  23.3 0.0 collective-permute-done.3.refs_3_
  23.3 0.0 collective-permute-done.4.refs_4_
  23.3 1.5 %collective-permute-done.5.refs_5_ = bf16[24,1280]{1,0:T(8,128)(2,1)S(1)} collective-permute-done((bf16[24,1280]{1,0:T(8,128)(2,1)S(1)}, bf16[24,1280]{1,0:T(8,128)(2,1)S(1)}, u32[]{:S(2)}, u32[]{:S(2)}) %collective-permute-start.5) | collective-permute-done | bytes 61472 | tf_op jit(solution)/shard_map/ppermute | solution.py:315
  24.8 0.3 %collective-permute-done.6.refs_6_ = bf16[24,1280]{1,0:T(8,128)(2,1)S(1)} collective-permute-done((bf16[24,1280]{1,0:T(8,128)(2,1)S(1)}, bf16[24,1280]{1,0:T(8,128)(2,1)S(1)}, u32[]{:S(2)}, u32[]{:S(2)}) %collective-permute-start.6) | collective-permute-done | bytes 61472 | tf_op jit(solution)/shard_map/ppermute | solution.py:315
  25.1 0.0 collective-permute-done.7.refs_7_
  25.1 1.2 %shard_map.95 = bf16[48,5120]{1,0:T(8,128)(2,1)} custom-call(bf16[192,192]{1,0:T(8,128)(2,1)S(1)} %get-tuple-element.18.place_ref, bf16[24,1280]{1,0:T(8,128)(2,1)S(1)} %get-tuple-element.23.refs_0_, bf16[24,1280]{1,0:T(8,128)(2,1)S(1)} %collective-permute-done.1.refs_1_, bf16[24,1280]{1,0:T(8,128)(2,1)S(1)} %collective-permute-done.2.refs_2_, ...), custom_call_target="tpu_custom_call" | custom-call | tf_op jit(solution)/shard_map/pallas_call | solution.py:322
Async XLA Ops:
  0.7 2.2 %copy-start = (bf16[1280,1280]{1,0:T(8,128)(2,1)S(1)}, bf16[1280,1280]{1,0:T(8,128)(2,1)}, u32[]{:S(2)}) copy-start(bf16[1280,1280]{1,0:T(8,128)(2,1)} %weight.1) | copy-start | bytes 9830404
  0.7 2.1 %copy-start.1 = (bf16[1280]{0:T(1024)(128)(2,1)S(1)}, bf16[1280]{0:T(1024)(128)(2,1)}, u32[]{:S(2)}) copy-start(bf16[1280]{0:T(1024)(128)(2,1)} %bias.1) | copy-start | bytes 7684
  0.7 2.1 %copy-start.2 = (bf16[1280]{0:T(1024)(128)(2,1)S(1)}, bf16[1280]{0:T(1024)(128)(2,1)}, u32[]{:S(2)}) copy-start(bf16[1280]{0:T(1024)(128)(2,1)} %gain.1) | copy-start | bytes 7684
  2.6 4.7 %copy-start.3 = (s32[1,48]{1,0:T(1,128)S(1)}, s32[1,48]{1,0:T(1,128)}, u32[]{:S(2)}) copy-start(s32[1,48]{1,0:T(1,128)} %slot_ref.1) | copy-start | bytes 580
  2.6 4.7 %copy-start.4 = (s32[1,48]{1,0:T(1,128)S(1)}, s32[1,48]{1,0:T(1,128)}, u32[]{:S(2)}) copy-start(s32[1,48]{1,0:T(1,128)} %row_ref.1) | copy-start | bytes 580
  3.6 8.1 %collective-permute-start = (bf16[64,1280]{1,0:T(8,128)(2,1)S(1)}, bf16[64,1280]{1,0:T(8,128)(2,1)S(1)}, u32[]{:S(2)}, u32[]{:S(2)}) collective-permute-start(bf16[64,1280]{1,0:T(8,128)(2,1)S(1)} %shard_map.93), channel_id=1, source_target_pairs={{24,0},{0,8},{8,16},{16,24},{25,1},{1,9},{9,17},{17,25},{26,2},{2,... | collective-permute-start | bytes 491528 | tf_op jit(solution)/shard_map/ppermute | solution.py:290
  12.0 6.7 %collective-permute-start.1 = (bf16[24,1280]{1,0:T(8,128)(2,1)S(1)}, bf16[24,1280]{1,0:T(8,128)(2,1)S(1)}, u32[]{:S(2)}, u32[]{:S(2)}) collective-permute-start(bf16[24,1280]{1,0:T(8,128)(2,1)S(1)} %get-tuple-element.24), channel_id=1, source_target_pairs={{0,4},{1,5},{2,6},{3,7},{4,0},{5,1},{6,2},{7,3},{8,12},{9,13},{10,... | collective-permute-start | bytes 184328 | tf_op jit(solution)/shard_map/ppermute | solution.py:315
  14.9 7.8 %collective-permute-start.2 = (bf16[24,1280]{1,0:T(8,128)(2,1)S(1)}, bf16[24,1280]{1,0:T(8,128)(2,1)S(1)}, u32[]{:S(2)}, u32[]{:S(2)}) collective-permute-start(bf16[24,1280]{1,0:T(8,128)(2,1)S(1)} %get-tuple-element.25), channel_id=1, source_target_pairs={{0,5},{1,4},{2,7},{3,6},{4,1},{5,0},{6,3},{7,2},{8,13},{9,12},{10,... | collective-permute-start | bytes 184328 | tf_op jit(solution)/shard_map/ppermute | solution.py:315
  14.9 8.5 %collective-permute-start.3 = (bf16[24,1280]{1,0:T(8,128)(2,1)S(1)}, bf16[24,1280]{1,0:T(8,128)(2,1)S(1)}, u32[]{:S(2)}, u32[]{:S(2)}) collective-permute-start(bf16[24,1280]{1,0:T(8,128)(2,1)S(1)} %get-tuple-element.26), channel_id=1, source_target_pairs={{0,2},{1,3},{2,4},{3,5},{4,6},{5,7},{6,0},{7,1},{8,10},{9,11},{10,... | collective-permute-start | bytes 184328 | tf_op jit(solution)/shard_map/ppermute | solution.py:315
  16.5 6.9 %collective-permute-start.4 = (bf16[24,1280]{1,0:T(8,128)(2,1)S(1)}, bf16[24,1280]{1,0:T(8,128)(2,1)S(1)}, u32[]{:S(2)}, u32[]{:S(2)}) collective-permute-start(bf16[24,1280]{1,0:T(8,128)(2,1)S(1)} %get-tuple-element.27), channel_id=1, source_target_pairs={{0,6},{1,7},{2,0},{3,1},{4,2},{5,3},{6,4},{7,5},{8,14},{9,15},{10,... | collective-permute-start | bytes 184328 | tf_op jit(solution)/shard_map/ppermute | solution.py:315
  18.7 6.1 %collective-permute-start.5 = (bf16[24,1280]{1,0:T(8,128)(2,1)S(1)}, bf16[24,1280]{1,0:T(8,128)(2,1)S(1)}, u32[]{:S(2)}, u32[]{:S(2)}) collective-permute-start(bf16[24,1280]{1,0:T(8,128)(2,1)S(1)} %get-tuple-element.28), channel_id=1, source_target_pairs={{0,3},{1,2},{2,5},{3,4},{4,7},{5,6},{6,1},{7,0},{8,11},{9,10},{10,... | collective-permute-start | bytes 184328 | tf_op jit(solution)/shard_map/ppermute | solution.py:315
  18.7 6.4 %collective-permute-start.6 = (bf16[24,1280]{1,0:T(8,128)(2,1)S(1)}, bf16[24,1280]{1,0:T(8,128)(2,1)S(1)}, u32[]{:S(2)}, u32[]{:S(2)}) collective-permute-start(bf16[24,1280]{1,0:T(8,128)(2,1)S(1)} %get-tuple-element.29), channel_id=1, source_target_pairs={{0,7},{1,6},{2,1},{3,0},{4,3},{5,2},{6,5},{7,4},{8,15},{9,14},{10,... | collective-permute-start | bytes 184328 | tf_op jit(solution)/shard_map/ppermute | solution.py:315
  22.7 2.4 %collective-permute-start.7 = (bf16[24,1280]{1,0:T(8,128)(2,1)S(1)}, bf16[24,1280]{1,0:T(8,128)(2,1)S(1)}, u32[]{:S(2)}, u32[]{:S(2)}) collective-permute-start(bf16[24,1280]{1,0:T(8,128)(2,1)S(1)} %get-tuple-element.30), channel_id=1, source_target_pairs={{0,1},{1,0},{2,3},{3,2},{4,5},{5,4},{6,7},{7,6},{8,9},{9,8},{10,11... | collective-permute-start | bytes 184328 | tf_op jit(solution)/shard_map/ppermute | solution.py:315
